TPU v7x, 512 devices: a whole 4x4x16 slice. The times are simulated.
512 devices in a mesh: section: 4 (over x), seq: 128 (over z, y, core).
Axes of the slice: x: 4, y: 4, z: 16, core: 2. Of those that a mesh axis runs over, the one named last changes fastest.
Arguments:
- feats: bfloat16 [4096, 8, 8, 768], P(('section', 'seq'))
- dw_weight: float32 [7, 7, 768], replicated, may hold values from -0.875 to 0.875
- dw_bias: float32 [768], replicated, may hold values from -3 to 3
- ln1_gain: float32 [768], replicated, may hold values from 0.5 to 2
- w_up: bfloat16 [1536, 768], P('section'), may hold values from -0.21875 to 0.21875
- b_up: bfloat16 [1536], P('section'), may hold values from -3 to 3
- w_down: bfloat16 [1536, 768], P('section'), may hold values from -0.15625 to 0.15625
- b_down: float32 [768], replicated, may hold values from -3 to 3
- layer_scale: float32 [768], replicated, may hold values from 0.3 to 1.5
- lnf_gain: float32 [768], replicated, may hold values from 0.5 to 2
- w_head: bfloat16 [768, 1536], P(None, 'section'), may hold values from -0.21875 to 0.21875
- prior: bfloat16 [77824, 1536], P(('section', 'seq')), may hold values from -6 to 6
- counts: int32 [512], P(('section', 'seq')), may hold values from 0 to 152, as said below
- positions: int32 [81920], P(('section', 'seq')), may hold values from 0 to 32767, as said below
- w_in: bfloat16 [1536, 768], P('section')
- ln_gain: float32 [768], replicated, may hold values from 0.5 to 2
- w_qkv: bfloat16 [768, 2304], P(None, 'section'), may hold values from -0.21875 to 0.21875
- qn_gain: float32 [64], replicated, may hold values from 0.5 to 2
- kn_gain: float32 [64], replicated, may hold values from 0.5 to 2
- offsets: int32 [12], replicated, may hold values from 0 to 15
- w_out: bfloat16 [768, 768], P('section'), may hold values from -6 to 6
Outputs:
- slide_out: bfloat16 [32768, 768], P('seq', 'section')
Inputs may be any that keep to these rules, and one draw needn't show every extreme that they name: `counts`: slot k of a device is valid when k < 8 + its count. Some device of every section index has count 152. `positions`: only valid slots' entries count. The valid slots of all devices hold every position 0 to 32767 exactly once; a valid slot of a device with section index s holds a position p with (p mod 256) div (64) = s. At most 2 valid slots of one device have the same p div 256, and some device reaches 2.
All inputs are finite; a program needn't handle non-finite values.
Results may differ from a plain program's by a relative error of at most 0.014.
Values may be sent and summed in bfloat16 or wider, within the bound.
No kernel may reach another device: no remote copies, remote signals or barrier semaphores. Data moves between devices by JAX's collectives and lax.ppermute only.
A program may use at most 64 MiB of HBM per device.

v0:
```python
import math
import jax
import jax.numpy as jnp
from jax import lax
from jax.sharding import PartitionSpec as P

HS = 64
RB = 16
ROWS = 256


def layer_norm(values, gain_vec):
    row_mean = jnp.mean(values, axis=-1, keepdims=True)
    centered = values - row_mean
    variance = jnp.mean(centered * centered, axis=-1, keepdims=True)
    return centered * lax.rsqrt(variance + 1e-06) * gain_vec


def rms_scale(values, gain_vec):
    return values * lax.rsqrt(jnp.mean(values * values, axis=-1, keepdims=True) + 1e-06) * gain_vec


def conv_norm(tile_maps, dw_weight, dw_bias, ln1_gain):
    map_side = tile_maps.shape[1]
    kernel = dw_weight.shape[0]
    half_width = (kernel - 1) // 2
    source = tile_maps.astype(jnp.float32)
    padded = jnp.pad(source, ((0, 0), (half_width, half_width), (half_width, half_width), (0, 0)))
    conv_sum = jnp.zeros_like(source) + dw_bias
    for row_off in range(kernel):
        for col_off in range(kernel):
            conv_sum = (
                conv_sum
                + padded[:, row_off : row_off + map_side, col_off : col_off + map_side, :]
                * dw_weight[row_off, col_off]
            )
    channels = source.shape[-1]
    normed_maps = layer_norm(conv_sum, ln1_gain).astype(jnp.bfloat16).reshape(-1, channels)
    return (source, normed_maps)


def pointwise(maps, up_rows, up_bias, down_rows, pixels):
    pre_act = lax.dot_general(
        maps, up_rows, (((1,), (1,)), ((), ())), preferred_element_type=jnp.float32
    ) + up_bias.astype(jnp.float32)
    hidden = jax.nn.gelu(pre_act, approximate=False).astype(jnp.bfloat16)
    branch = jnp.dot(hidden, down_rows, preferred_element_type=jnp.float32)
    return jnp.mean(branch.reshape(maps.shape[0] // pixels, pixels, branch.shape[1]), axis=1)


def shards(
    feats,
    dw_weight,
    dw_bias,
    ln1_gain,
    w_up,
    b_up,
    w_down,
    b_down,
    layer_scale,
    lnf_gain,
    w_head,
    prior,
    counts,
    positions,
    w_in,
    ln_gain,
    w_qkv,
    qn_gain,
    kn_gain,
    offsets,
    w_out,
):
    n_seq = lax.axis_size("seq")
    n_section = lax.axis_size("section")
    section_idx = lax.axis_index("section")
    pixels = feats.shape[1] * feats.shape[2]
    source, normed_maps = conv_norm(feats, dw_weight, dw_bias, ln1_gain)
    up_all, bias_all, down_all, head_all, in_all = (
        lax.all_gather(w_up, "section", axis=0, tiled=True),
        lax.all_gather(b_up, "section", axis=0, tiled=True),
        lax.all_gather(w_down, "section", axis=0, tiled=True),
        lax.all_gather(w_head, "section", axis=1, tiled=True),
        lax.all_gather(w_in, "section", axis=0, tiled=True),
    )
    branch_pooled = pointwise(normed_maps, up_all, bias_all, down_all, pixels)
    pooled = jnp.mean(source, axis=(1, 2)) + layer_scale * (branch_pooled + b_down)
    feature = layer_norm(pooled, lnf_gain).astype(jnp.bfloat16)
    fresh_emb = jnp.dot(feature, head_all, preferred_element_type=jnp.float32).astype(jnp.bfloat16)
    slot_rows = jnp.concatenate([fresh_emb, prior], axis=0)
    slot_total = slot_rows.shape[0]
    q_rows = ROWS // n_section
    capacity = -(-slot_total // n_seq)
    live_mask = jnp.arange(slot_total) < feats.shape[0] + counts[0]
    dest_shard = positions // ROWS
    row_in = positions % ROWS - section_idx * q_rows
    onehot_dest = jnp.logical_and(
        live_mask[:, None], dest_shard[:, None] == jnp.arange(n_seq)[None, :]
    ).astype(jnp.int32)
    before = jnp.cumsum(onehot_dest, axis=0) - onehot_dest
    within = jnp.sum(before * onehot_dest, axis=1)
    bucket = jnp.where(live_mask, dest_shard * capacity + within, -1)
    select = jnp.arange(n_seq * capacity)[:, None] == bucket[None, :]
    send_rows = (jnp.sum(jnp.where(select, row_in[None, :] + 1, 0), axis=1) - 1).reshape(
        n_seq, capacity
    )
    select_mat = select.astype(jnp.bfloat16)
    got_vals = lax.all_to_all(
        jnp.dot(select_mat, slot_rows, preferred_element_type=jnp.float32)
        .astype(jnp.bfloat16)
        .reshape(n_seq, capacity, slot_rows.shape[1]),
        "seq",
        split_axis=0,
        concat_axis=0,
        tiled=True,
    )
    got_rows = lax.all_to_all(send_rows, "seq", split_axis=0, concat_axis=0, tiled=True)
    flat_rows = got_rows.reshape(-1)
    placer = (jnp.arange(q_rows)[:, None] == flat_rows[None, :]).astype(jnp.bfloat16)
    x_local = jnp.dot(
        jnp.dot(
            placer,
            got_vals.reshape(flat_rows.shape[0], got_vals.shape[2]),
            preferred_element_type=jnp.float32,
        ).astype(jnp.bfloat16),
        in_all,
        preferred_element_type=jnp.float32,
    ).astype(jnp.bfloat16)
    x_rows = lax.all_gather(x_local, "section", axis=0, tiled=True)
    rows_total = x_rows.shape[0]
    normed = layer_norm(x_rows.astype(jnp.float32), ln_gain).astype(jnp.bfloat16)
    heads_here = w_qkv.shape[1] // (3 * HS)
    qkv_rows = (
        jnp.dot(normed, w_qkv, preferred_element_type=jnp.float32)
        .astype(jnp.bfloat16)
        .reshape(rows_total, 3, heads_here, HS)
    )
    queries = rms_scale(qkv_rows[:, 0].astype(jnp.float32), qn_gain).astype(jnp.bfloat16)
    keys_here = rms_scale(qkv_rows[:, 1].astype(jnp.float32), kn_gain).astype(jnp.bfloat16)
    values_here = qkv_rows[:, 2]
    score_scale = 1.0 / math.sqrt(HS)
    scores = (
        jnp.einsum("qhd,khd->hqk", queries, keys_here, preferred_element_type=jnp.float32)
        * score_scale
    )
    weights = jnp.exp(scores)
    local_den = jnp.sum(weights, axis=-1)
    local_num = jnp.einsum(
        "hqk,khd->hqd",
        weights.astype(jnp.bfloat16),
        values_here,
        preferred_element_type=jnp.float32,
    )
    my_offsets = lax.dynamic_slice_in_dim(offsets, section_idx * heads_here, heads_here)
    picker = jnp.arange(RB)[None, :] == my_offsets[:, None]
    pick_half = picker.astype(jnp.bfloat16)
    stride_rows = rows_total // RB

    def strided(matrix):
        return jnp.einsum(
            "arhd,hr->ahd",
            matrix.reshape(stride_rows, RB, heads_here, HS),
            pick_half,
            preferred_element_type=jnp.float32,
        ).astype(jnp.bfloat16)

    far_q = strided(queries)
    far_k = strided(keys_here)
    far_v = strided(values_here)
    piece_k = lax.all_gather(far_k, "seq", axis=0, tiled=True)
    piece_v = lax.all_gather(far_v, "seq", axis=0, tiled=True)
    far_scores = (
        jnp.einsum("ahd,bhd->hab", far_q, piece_k, preferred_element_type=jnp.float32) * score_scale
    )
    far_weights = jnp.exp(far_scores)
    far_add = jnp.einsum(
        "hab,bhd->had",
        far_weights.astype(jnp.bfloat16),
        piece_v,
        preferred_element_type=jnp.float32,
    )
    far_den = jnp.sum(far_weights, axis=-1)
    pick_full = picker.astype(jnp.float32)
    far_num_full = (far_add[:, :, None, :] * pick_full[:, None, :, None]).reshape(
        heads_here, rows_total, HS
    )
    far_den_full = (far_den[:, :, None] * pick_full[:, None, :]).reshape(heads_here, rows_total)
    attended = ((local_num + far_num_full) / (local_den + far_den_full)[:, :, None]).astype(
        jnp.bfloat16
    )
    merged = jnp.transpose(attended, (1, 0, 2)).reshape(rows_total, heads_here * HS)
    partial_out = jnp.dot(merged, w_out, preferred_element_type=jnp.float32)
    summed = lax.psum_scatter(partial_out, "section", scatter_dimension=1, tiled=True)
    width_part = summed.shape[1]
    residual = lax.dynamic_slice_in_dim(x_rows, section_idx * width_part, width_part, 1)
    return (residual.astype(jnp.float32) + summed).astype(jnp.bfloat16)


def solution(mesh):
    placed = (
        P(("section", "seq"), None, None, None),
        P(),
        P(),
        P(),
        P("section", None),
        P("section"),
        P("section", None),
        P(),
        P(),
        P(),
        P(None, "section"),
        P(("section", "seq"), None),
        P(("section", "seq")),
        P(("section", "seq")),
        P("section", None),
        P(),
        P(None, "section"),
        P(),
        P(),
        P(),
        P("section", None),
    )
    return jax.shard_map(
        shards, mesh=mesh, in_specs=placed, out_specs=P("seq", "section"), check_vma=False
    )
```

profile of v0, /device:TPU:8, one launch (start us, length us, event | category | flops | bytes accessed | tf_op | source)
XLA Modules:
  0.0 420.6 jit_solution(15630676997760096784)
XLA Ops:
  6.5 0.7 all-gather.6.cloned.1.call-update
  7.3 0.7 all-gather.8.cloned.1.call-update
  8.1 0.7 all-gather.10.cloned.1.call-update
  10.2 0.8 sub.50
  11.0 19.5 %all-to-all-start = ((s32[128,1,2]{2,1,0:T(1,128)}), s32[128,1,2]{2,1,0:T(1,128)S(1)}, u32[]{:S(2)}, u32[]{:S(2)}) async-start(s32[128,1,2]{2,1,0:T(1,128)} %bitcast.5), calls=%async_computation | async-start | bytes 131072 | tf_op jit(solution)/shard_map/all_to_all | solution.py:117
  32.2 9.5 %fusion.199 = (f32[8,8,8]{2,1,0:T(8,128)S(1)}, f32[8,8,8,768]{3,2,1,0:T(8,128)S(1)}) fusion(f32[768]{0:T(1024)S(1)} %get-tuple-element.54, f32[768]{0:T(1024)S(1)} %get-tuple-element.55, f32[768]{0:T(1024)S(1)} %get-tuple-element.8, f32[768]{0:T(1024)S(1)} %get-tuple-element.9, f32[768]{0:T(1024)S(1)} %get-tuple-element.10, f32[768]{0:T(1024)S(1)} %get-tuple-element.11, ...), kind=kLoop, calls=%fused_computation.360 | loop fusion | flops 38927872 | bytes 3301376 | tf_op jit(solution)/shard_map/reduce_sum | solution.py:13
  42.4 11.2 %all-gather = bf16[4,1,384]{2,1,0:T(2,128)(2,1)S(1)} all-gather(bf16[1,1,384]{2,1,0:T(2,128)(2,1)S(1)} %reshape.264), channel_id=1, replica_groups=mesh['section'=4,'seq'=128] {'section'}, dimensions={0}, use_global_device_ids=true | all-gather | bytes 3840 | tf_op jit(solution)/shard_map/all_gather | solution.py:81
  53.8 0.8 all-gather.6.cloned.1.call-done
  54.6 42.8 %all-gather.8.cloned.1.call-done = bf16[1536,768]{1,0:T(8,128)(2,1)} async-done(((bf16[384,768]{1,0:T(8,128)(2,1)}), bf16[1536,768]{1,0:T(8,128)(2,1)}) %all-gather.8.cloned.1.call-update) | async-done | bytes 2359312 | tf_op jit(solution)/shard_map/all_gather | solution.py:82
  97.5 11.2 %bitcast_reduce_fusion = f32[8,768]{1,0:T(8,128)S(1)} fusion(bf16[1536,768]{1,0:T(8,128)(2,1)} %all-gather.8.cloned.1.call-done, bf16[512,768]{1,0:T(8,128)(2,1)S(1)} %bitcast.95, bf16[1536,768]{1,0:T(8,128)(2,1)} %all-gather.6.cloned.1.call-done, f32[1536]{0:T(1024)S(1)} %reshape.266), kind=kOutput, calls=%fused_computation.170 | convolution fusion | flops 2468210688 | bytes 5535744 | tf_op jit(solution)/shard_map/dot_general | solution.py:47
  109.0 31.4 %all-gather.10.cloned.1.call-done = bf16[768,1536]{1,0:T(8,128)(2,1)} async-done(((bf16[768,384]{1,0:T(8,128)(2,1)}), bf16[768,1536]{1,0:T(8,128)(2,1)}) %all-gather.10.cloned.1.call-update) | async-done | bytes 2359312 | tf_op jit(solution)/shard_map/all_gather | solution.py:83
  140.5 2.1 convolution_convert_fusion.2
  143.1 1.2 reshape.255
  144.3 16.5 %all-to-all-start.1 = ((bf16[128,2,1536]{2,1,0:T(2,128)(2,1)}), bf16[128,2,1536]{2,1,0:T(2,128)(2,1)S(1)}, u32[]{:S(2)}, u32[]{:S(2)}) async-start(bf16[128,2,1536]{2,1,0:T(2,128)(2,1)} %reshape.255), calls=%async_computation.1 | async-start | bytes 1572864 | tf_op jit(solution)/shard_map/all_to_all | solution.py:108
  161.9 0.8 reduce.103
  162.8 39.8 %all-to-all-done.1 = bf16[128,2,1536]{2,1,0:T(2,128)(2,1)S(1)} async-done(((bf16[128,2,1536]{2,1,0:T(2,128)(2,1)}), bf16[128,2,1536]{2,1,0:T(2,128)(2,1)S(1)}, u32[]{:S(2)}, u32[]{:S(2)}) %all-to-all-start.1) | async-done | bytes 786464 | tf_op jit(solution)/shard_map/all_to_all | solution.py:108
  202.9 2.3 fusion.112
  205.3 13.0 %all_gather.29 = bf16[256,768]{1,0:T(8,128)(2,1)S(1)} all-gather(bf16[64,768]{1,0:T(8,128)(2,1)S(1)} %fusion.112), channel_id=1, replica_groups=mesh['section'=4,'seq'=128] {'section'}, dimensions={0}, use_global_device_ids=true | all-gather | bytes 491520 | tf_op jit(solution)/shard_map/all_gather | solution.py:129
  220.1 83.1 %all_gather.30 = bf16[2048,3,64]{2,0,1:T(8,128)(2,1)S(1)} all-gather(bf16[16,3,64]{2,0,1:T(8,128)(2,1)S(1)} %convert_bitcast_fusion.1), channel_id=1, replica_groups=mesh['section'=4,'seq'=128] {'seq'}, dimensions={0}, use_global_device_ids=true | all-gather | bytes 792576 | tf_op jit(solution)/shard_map/all_gather | solution.py:170
  305.0 83.0 %all_gather.31 = bf16[2048,3,64]{2,0,1:T(8,128)(2,1)S(1)} all-gather(bf16[16,3,64]{2,0,1:T(8,128)(2,1)S(1)} %convert_bitcast_fusion), channel_id=1, replica_groups=mesh['section'=4,'seq'=128] {'seq'}, dimensions={0}, use_global_device_ids=true | all-gather | bytes 792576 | tf_op jit(solution)/shard_map/all_gather | solution.py:171
  389.0 1.2 convolution_bitcast_fusion
  390.2 22.0 %reduce-scatter.4.cloned.1.call-done = f32[192,256]{1,0:T(8,128)} async-done(((f32[768,256]{1,0:T(8,128)}), f32[192,256]{1,0:T(8,128)}) %reduce-scatter.4.cloned.1.call-update) | async-done | bytes 196624
  412.2 1.1 copy.62
  413.4 0.7 copy.54
  (108 shorter events, 10.4 us)
Async XLA Ops:
  6.5 212.1 %copy-start = (bf16[768,576]{0,1:T(8,128)(2,1)S(1)}, bf16[768,576]{0,1:T(8,128)(2,1)}, u32[]{:S(2)}) copy-start(bf16[768,576]{0,1:T(8,128)(2,1)} %param.37) | copy-start | bytes 2654212
  6.5 2.9 copy-start.9
  6.5 48.1 %all-gather.6.cloned.1.call-start = ((), (), s32[]{:S(2)}) async-start(), calls=%async_computation.3 | async-start | bytes 2949120 | tf_op jit(solution)/shard_map/all_gather | solution.py:80
  7.3 23.8 %copy-start.3 = (f32[7,7,768]{2,1,0:T(8,128)S(1)}, f32[7,7,768]{2,1,0:T(8,128)}, u32[]{:S(2)}) copy-start(f32[7,7,768]{2,1,0:T(8,128)} %param.22) | copy-start | bytes 451588
  7.3 24.2 %copy-start.1 = (bf16[8,8,8,768]{3,2,1,0:T(8,128)(2,1)S(1)}, bf16[8,8,8,768]{3,2,1,0:T(8,128)(2,1)}, u32[]{:S(2)}) copy-start(bf16[8,8,8,768]{3,2,1,0:T(8,128)(2,1)} %param.21) | copy-start | bytes 2359300
  7.3 90.2 %all-gather.8.cloned.1.call-start = ((), (), s32[]{:S(2)}) async-start(), calls=%async_computation.4 | async-start | bytes 2949120 | tf_op jit(solution)/shard_map/all_gather | solution.py:82
  8.0 132.4 %all-gather.10.cloned.1.call-start = ((), (), s32[]{:S(2)}) async-start(), calls=%async_computation.5 | async-start | bytes 2949120 | tf_op jit(solution)/shard_map/all_gather | solution.py:83
  11.0 133.3 %all-to-all-start = ((s32[128,1,2]{2,1,0:T(1,128)}), s32[128,1,2]{2,1,0:T(1,128)S(1)}, u32[]{:S(2)}, u32[]{:S(2)}) async-start(s32[128,1,2]{2,1,0:T(1,128)} %bitcast.5), calls=%async_computation | async-start | bytes 131072 | tf_op jit(solution)/shard_map/all_to_all | solution.py:117
  30.5 172.5 %all-gather.12.cloned.1.call-start = ((), (), s32[]{:S(2)}) async-start(), calls=%async_computation.6 | async-start | bytes 2949120 | tf_op jit(solution)/shard_map/all_gather | solution.py:84
  31.5 0.7 copy-start.4
  41.7 0.7 copy-start.10
  41.7 11.9 %copy-start.5 = (f32[768]{0:T(1024)S(1)}, f32[768]{0:T(1024)}, u32[]{:S(2)}) copy-start(f32[768]{0:T(1024)} %param.24) | copy-start | bytes 9220
  97.5 11.2 %copy-start.7 = (f32[768]{0:T(1024)S(1)}, f32[768]{0:T(1024)}, u32[]{:S(2)}) copy-start(f32[768]{0:T(1024)} %param.28) | copy-start | bytes 9220
  97.5 11.2 %copy-start.8 = (f32[768]{0:T(1024)S(1)}, f32[768]{0:T(1024)}, u32[]{:S(2)}) copy-start(f32[768]{0:T(1024)} %param.29) | copy-start | bytes 9220
  97.5 43.0 %copy-start.6 = (f32[768]{0:T(1024)S(1)}, f32[768]{0:T(1024)}, u32[]{:S(2)}) copy-start(f32[768]{0:T(1024)} %param.30) | copy-start | bytes 9220
  108.7 33.9 %copy-start.13 = (bf16[152,1536]{1,0:T(8,128)(2,1)S(1)}, bf16[152,1536]{1,0:T(8,128)(2,1)}, u32[]{:S(2)}) copy-start(bf16[152,1536]{1,0:T(8,128)(2,1)} %param.32) | copy-start | bytes 1400836
  143.1 18.0 %copy-start.15 = (s32[12]{0:T(128)S(1)}, s32[12]{0:T(128)}, u32[]{:S(2)}) copy-start(s32[12]{0:T(128)} %param.40) | copy-start | bytes 148
  144.3 58.3 %all-to-all-start.1 = ((bf16[128,2,1536]{2,1,0:T(2,128)(2,1)}), bf16[128,2,1536]{2,1,0:T(2,128)(2,1)S(1)}, u32[]{:S(2)}, u32[]{:S(2)}) async-start(bf16[128,2,1536]{2,1,0:T(2,128)(2,1)} %reshape.255), calls=%async_computation.1 | async-start | bytes 1572864 | tf_op jit(solution)/shard_map/all_to_all | solution.py:108
  160.8 251.4 %reduce-scatter.4.cloned.1.call-start = ((), (), s32[]{:S(2)}) async-start(), calls=%async_computation.7 | async-start | bytes 983040
  202.9 15.7 %copy-start.14 = (f32[768]{0:T(1024)S(1)}, f32[768]{0:T(1024)}, u32[]{:S(2)}) copy-start(f32[768]{0:T(1024)} %param.36) | copy-start | bytes 9220
  219.2 0.7 copy-start.11
  219.3 83.9 %copy-start.12 = (f32[64]{0:T(128)S(1)}, f32[64]{0:T(128)}, u32[]{:S(2)}) copy-start(f32[64]{0:T(128)} %param.38) | copy-start | bytes 772
  388.0 1.0 copy-start.2
Sparse Core Ops, SparseCore 0:
  9.5 45.1 all-gather.5
  56.7 40.7 all-gather.7
  99.6 40.8 all-gather.9
  142.4 40.8 all-gather.11
  390.3 21.8 reduce-scatter.3
where the time goes:
time: 421 us
  blocking collectives  190 us (45%)
  waiting for transfers between devices  140 us (33%)
  starting transfers between devices  36.4 us (9%)
  matrix products  20.1 us (5%)
  between operations  14.2 us (3%)
  other arithmetic  12.9 us (3%)
  local copies, waits for them, and re-layouts  7.37 us (2%)
    all_gather x1, blocking collectives, shards(): piece_k = lax.all_gather(far_k, 'seq', axis=0, tiled=True)  83.1 us
    all_gather x1, blocking collectives, shards(): piece_v = lax.all_gather(far_v, 'seq', axis=0, tiled=True)  83 us
    all_gather x1, waiting for transfers between devices, shards(): lax.all_gather(w_down, 'section', axis=0, tiled=True)  42.8 us
    all_to_all x1, waiting for transfers between devices, shards(): lax.all_to_all(jnp.dot(select_mat, slot_rows, preferred_element_type=jnp....  39.8 us
    all_gather x1, waiting for transfers between devices, shards(): lax.all_gather(w_head, 'section', axis=1, tiled=True)  31.4 us
    unnamed x6, waiting for transfers between devices  24.6 us
    all_to_all x1, starting transfers between devices, shards(): lax.all_to_all(send_rows, 'seq', split_axis=0, concat_axis=0, tiled=True)  19.5 us
    all_to_all x1, starting transfers between devices, shards(): lax.all_to_all(jnp.dot(select_mat, slot_rows, preferred_element_type=jnp....  16.5 us
  transfers between devices with their start and end apart: 7, of which 5 were waited for; matrix products, arithmetic and copies ran while one was open for 7% of the time, Pallas kernels for 0%

commit v1 on v0

--- a/solution.py
+++ b/solution.py
@@ -167,8 +167,13 @@
     far_q = strided(queries)
     far_k = strided(keys_here)
     far_v = strided(values_here)
-    piece_k = lax.all_gather(far_k, "seq", axis=0, tiled=True)
-    piece_v = lax.all_gather(far_v, "seq", axis=0, tiled=True)
+    piece_k, piece_v = jnp.split(
+        jax.lax.all_gather(
+            jnp.concatenate([far_k, far_v], axis=1), axis_name="seq", axis=0, tiled=True
+        ),
+        [far_k.shape[1]],
+        axis=1,
+    )
     far_scores = (
         jnp.einsum("ahd,bhd->hab", far_q, piece_k, preferred_element_type=jnp.float32) * score_scale
     )

time: 421 us -> 390 us (0.926)
  blocking collectives: 190 us -> 24.1 us
  waiting for transfers between devices: 140 us -> 271 us
    all_gather x2 -> x0, blocking collectives: 166 us -> none  [the longest x1 83.1 us: shards(): piece_k = lax.all_gather(far_k, 'seq', axis=0, tiled=True)]
    all_gather x0 -> x1, waiting for transfers between devices: none -> 127 us  [shards(): jax.lax.all_gather(jnp.concatenate([far_k, far_v], axis=1), axis_name='se...]
    unnamed x6 -> x7, waiting for transfers between devices: 24.6 us -> 28.7 us
  transfers between devices with their start and end apart: 7 -> 8, of which waited for: 5 -> 6; matrix products, arithmetic and copies ran while one was open for 7% -> 8% of each run, Pallas kernels for 0% -> 0%
where the time goes in v1:
time: 390 us; the launch traced here: 389 us
  waiting for transfers between devices  271 us (69%)
  starting transfers between devices  36.4 us (9%)
  blocking collectives  24.1 us (6%)
  matrix products  23 us (6%)
  between operations  14.6 us (4%)
  other arithmetic  13.5 us (3%)
  local copies, waits for them, and re-layouts  7.14 us (2%)
    all_gather x1, waiting for transfers between devices, shards(): jax.lax.all_gather(jnp.concatenate([far_k, far_v], axis=1), axis_name='se...  127 us
    all_gather x1, waiting for transfers between devices, shards(): lax.all_gather(w_down, 'section', axis=0, tiled=True)  42.8 us
    all_to_all x1, waiting for transfers between devices, shards(): lax.all_to_all(jnp.dot(select_mat, slot_rows, preferred_element_type=jnp....  39.9 us
    all_gather x1, waiting for transfers between devices, shards(): lax.all_gather(w_head, 'section', axis=1, tiled=True)  31.4 us
    unnamed x7, waiting for transfers between devices  28.7 us
    all_to_all x1, starting transfers between devices, shards(): lax.all_to_all(send_rows, 'seq', split_axis=0, concat_axis=0, tiled=True)  19.5 us
    all_to_all x1, starting transfers between devices, shards(): lax.all_to_all(jnp.dot(select_mat, slot_rows, preferred_element_type=jnp....  16.5 us
    all_gather x1, blocking collectives, shards(): x_rows = lax.all_gather(x_local, 'section', axis=0, tiled=True)  13 us
  transfers between devices with their start and end apart: 8, of which 6 were waited for; matrix products, arithmetic and copies ran while one was open for 8% of the time, Pallas kernels for 0%

profile of v1, /device:TPU:8, one launch (start us, length us, event | category | flops | bytes accessed | tf_op | source)
XLA Modules:
  0.0 389.3 jit_solution(4346700646325529707)
XLA Ops:
  6.5 0.7 all-gather.7.cloned.1.call-update
  7.3 0.7 all-gather.9.cloned.1.call-update
  10.2 0.8 sub.50
  11.0 19.5 %all-to-all-start = ((s32[128,1,2]{2,1,0:T(1,128)}), s32[128,1,2]{2,1,0:T(1,128)S(1)}, u32[]{:S(2)}, u32[]{:S(2)}) async-start(s32[128,1,2]{2,1,0:T(1,128)} %bitcast.5), calls=%async_computation | async-start | bytes 131072 | tf_op jit(solution)/shard_map/all_to_all | solution.py:117
  32.2 9.5 %fusion.201 = (f32[8,8,8]{2,1,0:T(8,128)S(1)}, f32[8,8,8,768]{3,2,1,0:T(8,128)S(1)}) fusion(f32[768]{0:T(1024)S(1)} %get-tuple-element.54, f32[768]{0:T(1024)S(1)} %get-tuple-element.55, f32[768]{0:T(1024)S(1)} %get-tuple-element.8, f32[768]{0:T(1024)S(1)} %get-tuple-element.9, f32[768]{0:T(1024)S(1)} %get-tuple-element.10, f32[768]{0:T(1024)S(1)} %get-tuple-element.11, ...), kind=kLoop, calls=%fused_computation.363 | loop fusion | flops 38927872 | bytes 3301376 | tf_op jit(solution)/shard_map/reduce_sum | solution.py:13
  42.4 11.2 %all-gather = bf16[4,1,384]{2,1,0:T(2,128)(2,1)S(1)} all-gather(bf16[1,1,384]{2,1,0:T(2,128)(2,1)S(1)} %reshape.264), channel_id=1, replica_groups=mesh['section'=4,'seq'=128] {'section'}, dimensions={0}, use_global_device_ids=true | all-gather | bytes 3840 | tf_op jit(solution)/shard_map/all_gather | solution.py:81
  53.8 0.8 all-gather.7.cloned.1.call-done
  54.6 42.8 %all-gather.9.cloned.1.call-done = bf16[1536,768]{1,0:T(8,128)(2,1)} async-done(((bf16[384,768]{1,0:T(8,128)(2,1)}), bf16[1536,768]{1,0:T(8,128)(2,1)}) %all-gather.9.cloned.1.call-update) | async-done | bytes 2359312 | tf_op jit(solution)/shard_map/all_gather | solution.py:82
  97.5 11.2 %bitcast_reduce_fusion = f32[8,768]{1,0:T(8,128)S(1)} fusion(bf16[1536,768]{1,0:T(8,128)(2,1)} %all-gather.9.cloned.1.call-done, bf16[512,768]{1,0:T(8,128)(2,1)S(1)} %bitcast.93, bf16[1536,768]{1,0:T(8,128)(2,1)} %all-gather.7.cloned.1.call-done, f32[1536]{0:T(1024)S(1)} %reshape.266), kind=kOutput, calls=%fused_computation.173 | convolution fusion | flops 2468210688 | bytes 5535744 | tf_op jit(solution)/shard_map/dot_general | solution.py:47
  109.0 31.4 %all-gather.11.cloned.1.call-done = bf16[768,1536]{1,0:T(8,128)(2,1)} async-done(((bf16[768,384]{1,0:T(8,128)(2,1)}), bf16[768,1536]{1,0:T(8,128)(2,1)}) %all-gather.11.cloned.1.call-update) | async-done | bytes 2359312 | tf_op jit(solution)/shard_map/all_gather | solution.py:83
  140.5 2.1 convolution_convert_fusion.2
  143.1 1.2 reshape.255
  144.3 16.5 %all-to-all-start.1 = ((bf16[128,2,1536]{2,1,0:T(2,128)(2,1)}), bf16[128,2,1536]{2,1,0:T(2,128)(2,1)S(1)}, u32[]{:S(2)}, u32[]{:S(2)}) async-start(bf16[128,2,1536]{2,1,0:T(2,128)(2,1)} %reshape.255), calls=%async_computation.1 | async-start | bytes 1572864 | tf_op jit(solution)/shard_map/all_to_all | solution.py:108
  161.8 0.8 reduce.103
  162.7 39.9 %all-to-all-done.1 = bf16[128,2,1536]{2,1,0:T(2,128)(2,1)S(1)} async-done(((bf16[128,2,1536]{2,1,0:T(2,128)(2,1)}), bf16[128,2,1536]{2,1,0:T(2,128)(2,1)S(1)}, u32[]{:S(2)}, u32[]{:S(2)}) %all-to-all-start.1) | async-done | bytes 786464 | tf_op jit(solution)/shard_map/all_to_all | solution.py:108
  202.9 2.3 fusion.115
  205.3 13.0 %all_gather.26 = bf16[256,768]{1,0:T(8,128)(2,1)S(1)} all-gather(bf16[64,768]{1,0:T(8,128)(2,1)S(1)} %fusion.115), channel_id=1, replica_groups=mesh['section'=4,'seq'=128] {'section'}, dimensions={0}, use_global_device_ids=true | all-gather | bytes 491520 | tf_op jit(solution)/shard_map/all_gather | solution.py:129
  222.0 126.9 %all-gather.15.cloned.1.call-done = bf16[2048,6,64]{2,0,1:T(8,128)(2,1)} async-done(((bf16[16,6,64]{2,0,1:T(8,128)(2,1)}), bf16[2048,6,64]{2,0,1:T(8,128)(2,1)}) %all-gather.15.cloned.1.call-update) | async-done | bytes 1572880 | tf_op jit(solution)/shard_map/all_gather | solution.py:171
  348.8 2.0 fusion.204
  351.0 1.8 fusion.108
  353.2 1.2 convolution_bitcast_fusion
  354.5 26.1 %reduce-scatter.4.cloned.1.call-done = f32[192,256]{1,0:T(8,128)} async-done(((f32[768,256]{1,0:T(8,128)}), f32[192,256]{1,0:T(8,128)}) %reduce-scatter.4.cloned.1.call-update) | async-done | bytes 196624
  380.5 1.1 copy.66
  381.7 0.7 copy.58
  (110 shorter events, 10.7 us)
Async XLA Ops:
  6.5 212.1 %copy-start = (bf16[768,576]{0,1:T(8,128)(2,1)S(1)}, bf16[768,576]{0,1:T(8,128)(2,1)}, u32[]{:S(2)}) copy-start(bf16[768,576]{0,1:T(8,128)(2,1)} %param.37) | copy-start | bytes 2654212
  6.5 2.9 copy-start.9
  6.5 48.1 %all-gather.7.cloned.1.call-start = ((), (), s32[]{:S(2)}) async-start(), calls=%async_computation.3 | async-start | bytes 2949120 | tf_op jit(solution)/shard_map/all_gather | solution.py:80
  7.3 23.8 %copy-start.3 = (f32[7,7,768]{2,1,0:T(8,128)S(1)}, f32[7,7,768]{2,1,0:T(8,128)}, u32[]{:S(2)}) copy-start(f32[7,7,768]{2,1,0:T(8,128)} %param.22) | copy-start | bytes 451588
  7.3 24.2 %copy-start.1 = (bf16[8,8,8,768]{3,2,1,0:T(8,128)(2,1)S(1)}, bf16[8,8,8,768]{3,2,1,0:T(8,128)(2,1)}, u32[]{:S(2)}) copy-start(bf16[8,8,8,768]{3,2,1,0:T(8,128)(2,1)} %param.21) | copy-start | bytes 2359300
  7.3 90.2 %all-gather.9.cloned.1.call-start = ((), (), s32[]{:S(2)}) async-start(), calls=%async_computation.4 | async-start | bytes 2949120 | tf_op jit(solution)/shard_map/all_gather | solution.py:82
  8.0 132.4 %all-gather.11.cloned.1.call-start = ((), (), s32[]{:S(2)}) async-start(), calls=%async_computation.5 | async-start | bytes 2949120 | tf_op jit(solution)/shard_map/all_gather | solution.py:83
  11.0 133.3 %all-to-all-start = ((s32[128,1,2]{2,1,0:T(1,128)}), s32[128,1,2]{2,1,0:T(1,128)S(1)}, u32[]{:S(2)}, u32[]{:S(2)}) async-start(s32[128,1,2]{2,1,0:T(1,128)} %bitcast.5), calls=%async_computation | async-start | bytes 131072 | tf_op jit(solution)/shard_map/all_to_all | solution.py:117
  30.5 172.5 %all-gather.13.cloned.1.call-start = ((), (), s32[]{:S(2)}) async-start(), calls=%async_computation.6 | async-start | bytes 2949120 | tf_op jit(solution)/shard_map/all_gather | solution.py:84
  31.5 0.7 copy-start.4
  41.7 0.7 copy-start.10
  41.7 11.9 %copy-start.5 = (f32[768]{0:T(1024)S(1)}, f32[768]{0:T(1024)}, u32[]{:S(2)}) copy-start(f32[768]{0:T(1024)} %param.24) | copy-start | bytes 9220
  97.5 11.2 %copy-start.7 = (f32[768]{0:T(1024)S(1)}, f32[768]{0:T(1024)}, u32[]{:S(2)}) copy-start(f32[768]{0:T(1024)} %param.28) | copy-start | bytes 9220
  97.5 11.2 %copy-start.8 = (f32[768]{0:T(1024)S(1)}, f32[768]{0:T(1024)}, u32[]{:S(2)}) copy-start(f32[768]{0:T(1024)} %param.29) | copy-start | bytes 9220
  97.5 43.0 %copy-start.6 = (f32[768]{0:T(1024)S(1)}, f32[768]{0:T(1024)}, u32[]{:S(2)}) copy-start(f32[768]{0:T(1024)} %param.30) | copy-start | bytes 9220
  108.7 33.9 %copy-start.13 = (bf16[152,1536]{1,0:T(8,128)(2,1)S(1)}, bf16[152,1536]{1,0:T(8,128)(2,1)}, u32[]{:S(2)}) copy-start(bf16[152,1536]{1,0:T(8,128)(2,1)} %param.32) | copy-start | bytes 1400836
  143.1 18.0 %copy-start.15 = (s32[12]{0:T(128)S(1)}, s32[12]{0:T(128)}, u32[]{:S(2)}) copy-start(s32[12]{0:T(128)} %param.40) | copy-start | bytes 148
  144.3 58.3 %all-to-all-start.1 = ((bf16[128,2,1536]{2,1,0:T(2,128)(2,1)}), bf16[128,2,1536]{2,1,0:T(2,128)(2,1)S(1)}, u32[]{:S(2)}, u32[]{:S(2)}) async-start(bf16[128,2,1536]{2,1,0:T(2,128)(2,1)} %reshape.255), calls=%async_computation.1 | async-start | bytes 1572864 | tf_op jit(solution)/shard_map/all_to_all | solution.py:108
  160.8 188.0 %all-gather.15.cloned.1.call-start = ((), (), s32[]{:S(2)}) async-start(), calls=%async_computation.7 | async-start | bytes 3170304 | tf_op jit(solution)/shard_map/all_gather | solution.py:171
  202.9 15.7 %copy-start.14 = (f32[768]{0:T(1024)S(1)}, f32[768]{0:T(1024)}, u32[]{:S(2)}) copy-start(f32[768]{0:T(1024)} %param.36) | copy-start | bytes 9220
  218.6 0.9 copy-start.11
  219.2 2.1 copy-start.12
  220.9 159.7 %reduce-scatter.4.cloned.1.call-start = ((), (), s32[]{:S(2)}) async-start(), calls=%async_computation.8 | async-start | bytes 983040
  351.0 2.2 copy-start.2
Sparse Core Ops, SparseCore 0:
  9.5 45.1 all-gather.6
  56.7 40.7 all-gather.8
  99.6 40.8 all-gather.10
  142.4 40.8 all-gather.12
  221.0 127.8 all-gather.14
  354.6 25.8 reduce-scatter.3
